TPU v7x, 32 devices: a whole 2x2x4 slice. The times are simulated.
32 devices in a mesh: mic: 16 (over z, y, x), seg: 2 (over core).
Axes of the slice: x: 2, y: 2, z: 4, core: 2. Of those that a mesh axis runs over, the one named last changes fastest.
Arguments:
- pressure: bfloat16 [2, 4, 64, 8192], P(None, None, 'seg', 'mic'), may hold values from -6 to 6
- harmonics: bfloat16 [8192, 4096], P('mic'), may hold values from -0.0625 to 0.0625
- steering: bfloat16 [4096, 2048], P(None, 'mic'), may hold values from -0.09375 to 0.09375
- radial_mag: float32 [4, 64], replicated, may hold values from 0.5 to 2
- radial_phase: float32 [4, 64], replicated, may hold values from -3.140625 to 3.140625
- noise: float32 [4, 4096], replicated, may hold values from 0.5 to 8
Outputs:
- beam_power: float32 [4, 2048], P(None, 'mic')
All inputs are finite; a program needn't handle non-finite values.
Results may differ from a plain program's by a relative error of at most 0.00057.
Values may be sent and summed in bfloat16 or wider, within the bound.
A program may use at most 64 MiB of HBM per device.

v0:
```python
import jax
import jax.numpy as jnp
from jax import lax
from jax.sharding import PartitionSpec as P


def order_lookup(table, count, start):
    orders = table.shape[1]
    index = start + jnp.arange(count, dtype=jnp.int32)
    squares = jnp.arange(1, orders, dtype=jnp.int32) ** 2
    level = jnp.sum((index[:, None] >= squares[None, :]).astype(jnp.int32), axis=1)
    select = level[:, None] == jnp.arange(orders, dtype=jnp.int32)[None, :]
    return jnp.sum(jnp.where(select[:, None, :], table[None, :, :], jnp.float32(0.0)), axis=2)


def shards(pressure, harmonics, steering, radial_mag, radial_phase, noise):
    bins = pressure.shape[1]
    seg_local = pressure.shape[2]
    mic_local = pressure.shape[3]
    rows = 2 * bins * seg_local
    segments = seg_local * lax.axis_size("seg")
    flat = pressure.reshape(rows, mic_local)
    local_terms = lax.dot_general(
        harmonics, flat, (((0,), (1,)), ((), ())), preferred_element_type=jnp.float32
    )
    owned = lax.psum(local_terms, "mic")
    first = 0
    count = owned.shape[0]
    coeff = owned.reshape(count, 2, bins, seg_local)
    local_power = jnp.sum(coeff[:, 0] * coeff[:, 0] + coeff[:, 1] * coeff[:, 1], axis=2)
    power = lax.psum(local_power, "seg") / segments
    noise_part = noise.T
    mag = order_lookup(radial_mag, count, first)
    phi = order_lookup(radial_phase, count, first)
    gain = (power / (power + noise_part) / mag)[:, :, None]
    cosine = jnp.cos(phi)[:, :, None]
    sine = jnp.sin(phi)[:, :, None]
    real_part = gain * (coeff[:, 0] * cosine + coeff[:, 1] * sine)
    imag_part = gain * (coeff[:, 1] * cosine - coeff[:, 0] * sine)
    equalized = jnp.stack([real_part, imag_part], axis=1).astype(jnp.bfloat16).reshape(count, rows)
    beam = lax.dot_general(
        steering, equalized, (((0,), (0,)), ((), ())), preferred_element_type=jnp.float32
    )
    beam = beam.reshape(steering.shape[1], 2, bins, seg_local)
    local_beam = jnp.sum(beam[:, 0] * beam[:, 0] + beam[:, 1] * beam[:, 1], axis=2)
    total = lax.psum(local_beam, "seg") / segments
    return total.T


def solution(mesh):
    placed = (P(None, None, "seg", "mic"), P("mic", None), P(None, "mic"), P(), P(), P())
    return jax.shard_map(
        shards, mesh=mesh, in_specs=placed, out_specs=P(None, "mic"), check_vma=False
    )
```

profile of v0, /device:TPU:1, one launch (start us, length us, event | category | flops | bytes accessed | tf_op | source)
XLA Modules:
  0.0 218.4 jit_solution(3374588451856649891)
XLA Ops:
  6.5 0.0 copy-start
  6.5 0.0 all-reduce.3.cloned.1.call-start
  6.5 5.6 %fusion.6 = f32[4096,256]{0,1:T(8,128)} fusion(bf16[256,512]{1,0:T(8,128)(2,1)} %bitcast.20, bf16[512,4096]{1,0:T(8,128)(2,1)} %param.7), kind=kOutput, calls=%fused_computation.20 | convolution fusion | flops 1073741824 | bytes 8650752 | tf_op jit(solution)/shard_map/dot_general | solution.py:23
  12.1 0.0 all-reduce.3.cloned.1.call-update
  12.2 0.0 all-reduce.5.cloned.1.call-start
  12.2 0.2 convert_reduce_fusion
  12.4 0.1 iota_compare_fusion
  12.6 0.2 copy-done.2
  12.8 0.0 copy-done.3
  12.8 0.9 select_reduce_fusion.1
  13.7 0.0 copy-start.1
  13.8 169.5 %all-reduce.3.cloned.1.call-done = f32[4096,2,4,32]{0,3,2,1:T(8,128)} async-done(((f32[4096,2,4,32]{0,3,2,1:T(8,128)}), f32[4096,2,4,32]{0,3,2,1:T(8,128)}) %all-reduce.3.cloned.1.call-update) | async-done | bytes 4194320 | tf_op jit(solution)/shard_map/psum | solution.py:26
  183.3 3.3 %add_reduce_fusion = f32[4096,4]{0,1:T(4,128)} fusion(f32[4096,2,4,32]{0,3,2,1:T(8,128)} %all-reduce.3.cloned.1.call-done), kind=kLoop, calls=%fused_computation.5 | loop fusion | flops 2080768 | bytes 4259840 | tf_op jit(solution)/shard_map/reduce_sum | solution.py:30
  186.6 0.0 all-reduce.5.cloned.1.call-update
  186.6 0.5 fusion.4
  187.1 16.7 %all-reduce.5.cloned.1.call-done = f32[4096,4]{0,1:T(4,128)} async-done(((f32[4096,4]{0,1:T(4,128)}), f32[4096,4]{0,1:T(4,128)}) %all-reduce.5.cloned.1.call-update) | async-done | bytes 65552 | tf_op jit(solution)/shard_map/psum | solution.py:31
  203.8 0.0 copy-done.1
  203.8 0.9 fusion.3
  204.7 2.9 %multiply_convert_fusion.1 = (bf16[4096,1,4,32]{0,3,2,1:T(8,128)(2,1)S(1)}, bf16[4096,1,4,32]{0,3,2,1:T(8,128)(2,1)S(1)}) fusion(f32[4096,2,4,32]{0,3,2,1:T(8,128)} %all-reduce.3.cloned.1.call-done, f32[4096,4]{0,1:T(4,128)S(1)} %get-tuple-element.10, f32[4096,4]{0,1:T(4,128)S(1)} %get-tuple-element.9, f32[4096,4]{0,1:T(4,128)S(1)} %fusion.3), kind=kLoop, calls=%fused_computation.4 | loop fusion | flops 5242880 | bytes 6488064 | tf_op jit(solution)/shard_map/convert
  207.6 0.2 pad_maximum_fusion
  207.8 0.0 copy-done
  207.8 0.7 fusion.5
  208.5 2.5 %psum.23 = f32[128,4]{0,1:T(4,128)S(1)} all-reduce(f32[128,4]{0,1:T(4,128)S(1)} %fusion.1), channel_id=1, replica_groups=mesh['mic'=16,'seg'=2] {'seg'}, use_global_device_ids=true, to_apply=%region_7.8 | all-reduce | flops 512 | bytes 4096 | tf_op jit(solution)/shard_map/psum | solution.py:46
  211.0 0.6 multiply_bitcast_fusion
  (4 shorter events, 0.0 us)
Async XLA Ops:
  6.5 201.2 %copy-start = (bf16[4096,128]{1,0:T(8,128)(2,1)S(1)}, bf16[4096,128]{1,0:T(8,128)(2,1)}, u32[]{:S(2)}) copy-start(bf16[4096,128]{1,0:T(8,128)(2,1)} %param.8) | copy-start | bytes 3145732
  6.5 176.7 %all-reduce.3.cloned.1.call-start = ((), (), s32[]{:S(2)}) async-start(), calls=%async_computation | async-start | bytes 8388608 | tf_op jit(solution)/shard_map/psum | solution.py:26
  12.1 0.7 copy-start.2
  12.1 0.7 copy-start.3
  12.2 191.7 %all-reduce.5.cloned.1.call-start = ((), (), s32[]{:S(2)}) async-start(), calls=%async_computation.1 | async-start | bytes 131072 | tf_op jit(solution)/shard_map/psum | solution.py:31
  13.7 190.1 %copy-start.1 = (f32[4,4096]{1,0:T(4,128)S(1)}, f32[4,4096]{1,0:T(4,128)}, u32[]{:S(2)}) copy-start(f32[4,4096]{1,0:T(4,128)} %param.11) | copy-start | bytes 196612
Sparse Core Ops, SparseCore 0:
  13.0 170.2 all-reduce.2
  186.8 17.0 all-reduce.4
where the time goes:
time: 219 us; the launch traced here: 218 us
  waiting for transfers between devices  186 us (85%)
  between operations  13.5 us (6%)
  other arithmetic  9.14 us (4%)
  matrix products  6.31 us (3%)
  blocking collectives  2.48 us (1%)
    psum x1, waiting for transfers between devices, shards(): owned = lax.psum(local_terms, 'mic')  170 us
    psum x1, waiting for transfers between devices, shards(): power = lax.psum(local_power, 'seg') / segments  16.7 us
    dot_general x1, matrix products, shards(): lax.dot_general(harmonics, flat, (((0,), (1,)), ((), ())), preferred_elem...  5.58 us
  transfers between devices with their start and end apart: 2, of which 2 were waited for; matrix products, arithmetic and copies ran while one was open for 1% of the time, Pallas kernels for 0%

commit v1 on v0

--- a/solution.py
+++ b/solution.py
@@ -1,7 +1,15 @@
+import functools
+
 import jax
 import jax.numpy as jnp
 from jax import lax
+from jax.experimental import pallas as pl
+from jax.experimental.pallas import tpu as pltpu
 from jax.sharding import PartitionSpec as P
+
+MESH = pl.DeviceIdType.MESH
+HALF = 128
+OFFSET = 2.5
 
 
 def order_lookup(table, count, start):
@@ -16,20 +24,19 @@
 def shards(pressure, harmonics, steering, radial_mag, radial_phase, noise):
     bins = pressure.shape[1]
     seg_local = pressure.shape[2]
-    mic_local = pressure.shape[3]
     rows = 2 * bins * seg_local
     segments = seg_local * lax.axis_size("seg")
-    flat = pressure.reshape(rows, mic_local)
+    flat = pressure.reshape(rows, pressure.shape[3])
     local_terms = lax.dot_general(
         harmonics, flat, (((0,), (1,)), ((), ())), preferred_element_type=jnp.float32
     )
-    owned = lax.psum(local_terms, "mic")
-    first = 0
+    owned = lax.psum_scatter(local_terms, "mic", scatter_dimension=0, tiled=True)
     count = owned.shape[0]
+    first = lax.axis_index("mic") * count
     coeff = owned.reshape(count, 2, bins, seg_local)
     local_power = jnp.sum(coeff[:, 0] * coeff[:, 0] + coeff[:, 1] * coeff[:, 1], axis=2)
     power = lax.psum(local_power, "seg") / segments
-    noise_part = noise.T
+    noise_part = lax.dynamic_slice_in_dim(noise, first, count, 1).T
     mag = order_lookup(radial_mag, count, first)
     phi = order_lookup(radial_phase, count, first)
     gain = (power / (power + noise_part) / mag)[:, :, None]
@@ -38,6 +45,7 @@
     real_part = gain * (coeff[:, 0] * cosine + coeff[:, 1] * sine)
     imag_part = gain * (coeff[:, 1] * cosine - coeff[:, 0] * sine)
     equalized = jnp.stack([real_part, imag_part], axis=1).astype(jnp.bfloat16).reshape(count, rows)
+    equalized = lax.all_gather(equalized, "mic", axis=0, tiled=True)
     beam = lax.dot_general(
         steering, equalized, (((0,), (0,)), ((), ())), preferred_element_type=jnp.float32
     )
@@ -47,8 +55,263 @@
     return total.T
 
 
+def encode(value):
+    square = value * value
+    return (square * (value * jnp.abs(value))).astype(jnp.bfloat16)
+
+
+def decode(code):
+    code = code.astype(jnp.float32)
+    size = jnp.abs(code)
+    root = lax.rsqrt(lax.rsqrt(jnp.maximum(size, 1e-37)))
+    return jnp.where(code < 0, -root, jnp.where(code > 0, root, 0.0))
+
+
+def schedule(bins, bits):
+    length = [2.6] + [2.0] + [1.5] * (bits - 2)
+    after = length + [1.5] + length[::-1]
+    at, events = 0.0, []
+    for step in range(len(after) + 1):
+        for b in range(bins):
+            events.append((at + OFFSET * b, -step, b))
+        if step < len(after):
+            at += after[step]
+    return [(b, -negative) for _, negative, b in sorted(events)]
+
+
+def kernel(
+    n, bits, seg_local,
+    pressure, harmonics, steering, mag, phase, noise, out,
+    pbuf, hbuf, sbuf, tables, acc, code_out, code_in, gathered,
+    power_out, power_in, beam_out, beam_in,
+    local_sem, rs_send, rs_recv, ag_send, ag_recv, pw_send, pw_recv, bm_send, bm_recv,
+):
+    bins, orders_count = mag.shape
+    rows = 2 * seg_local
+    segments = seg_local * 2
+    me, core = lax.axis_index("mic"), lax.axis_index("seg")
+    step_of = [(1 << b) * (1 - 2 * ((me // (1 << b)) % 2)) for b in range(bits)]
+    orders = ([0, 1] + list(range(2, bits)), [1, 0] + list(range(2, bits)))
+
+    def owner(r):
+        return me + sum(step_of[b] for b in range(bits) if (r >> b) & 1)
+
+    def slot(h, r):
+        return sum(((r >> b) & 1) << (bits - 1 - j) for j, b in enumerate(orders[h]))
+
+    def near(bit):
+        return (me + step_of[bit], core)
+
+    other = (me, 1 - core)
+
+    sequence = sorted(range(n), key=lambda r: (-(r & 1), -(r & 2), r))
+    width = 2 * HALF
+    loads = {"p": pltpu.make_async_copy(pressure, pbuf, local_sem.at[0])}
+    loads["p"].start()
+    for r in sequence:
+        first = pl.multiple_of(owner(r) * width, width)
+        loads["h", r] = pltpu.make_async_copy(
+            harmonics.at[:, pl.ds(first, width)], hbuf.at[r], local_sem.at[1 + r]
+        )
+        loads["h", r].start()
+    barrier = pltpu.get_barrier_semaphore()
+    for b in range(bits):
+        pl.semaphore_signal(barrier, inc=1, device_id=near(b), device_id_type=MESH)
+    pl.semaphore_signal(barrier, inc=1, device_id=other, device_id_type=MESH)
+    for r in range(n):
+        first = pl.multiple_of(owner(r) * width, width)
+        loads["s", r] = pltpu.make_async_copy(
+            steering.at[pl.ds(first, width), :], sbuf.at[r], local_sem.at[1 + n + r]
+        )
+        loads["s", r].start()
+
+    sends = []
+
+    def remote(src, dst, send_sem, recv_sem, device):
+        copy = pltpu.make_async_remote_copy(
+            src_ref=src, dst_ref=dst, send_sem=send_sem, recv_sem=recv_sem,
+            device_id=device, device_id_type=MESH,
+        )
+        copy.start()
+        sends.append(copy)
+        return copy
+
+    scatter, gather, powers = {}, {}, {}
+
+    def send_scatter(b, h, j):
+        half = 1 << (bits - 1 - j)
+        scatter[b, h, j] = remote(
+            code_out.at[b, h, pl.ds(half, half)], code_in.at[b, h, pl.ds(half, half)],
+            rs_send.at[b, h, j], rs_recv.at[b, h, j], near(orders[h][j]),
+        )
+
+    def send_gather(b, h, j):
+        half = 1 << (bits - 1 - j)
+        gather[b, h, j] = remote(
+            gathered.at[b, h, pl.ds(0, half)], gathered.at[b, h, pl.ds(half, half)],
+            ag_send.at[b, h, j], ag_recv.at[b, h, j], near(orders[h][j]),
+        )
+
+    events = schedule(bins, bits)
+    early = 0
+    while events[early][1] == 0:
+        early += 1
+
+    loads["p"].wait()
+    for count, r in enumerate(sequence):
+        loads["h", r].wait()
+        part = jnp.dot(pbuf[...], hbuf[r], preferred_element_type=jnp.float32)
+        for h in range(2):
+            where = slot(h, r)
+            for b in range(bins):
+                for c in range(2):
+                    first = (c * bins + b) * seg_local
+                    block = part[first:first + seg_local, h * HALF:(h + 1) * HALF]
+                    if where >= n // 2:
+                        code_out[b, h, where, c * seg_local:(c + 1) * seg_local, :] = encode(block)
+                    else:
+                        acc[b, h, where, c * seg_local:(c + 1) * seg_local, :] = block
+        if count == n // 2 - 1:
+            pl.semaphore_wait(barrier, bits + 1)
+            for b, _ in events[:early]:
+                send_scatter(b, 0, 0)
+        if count == 3 * n // 4 - 1:
+            for b, _ in events[:early]:
+                send_scatter(b, 1, 0)
+
+    index = me * width + lax.broadcasted_iota(jnp.int32, (orders_count, width), 1)
+    order = lax.broadcasted_iota(jnp.int32, (orders_count, width), 0)
+    last = order == orders_count - 1
+    select = (index >= order * order) & ((index < (order + 1) * (order + 1)) | last)
+    chosen = jnp.where(select, 1.0, 0.0).astype(jnp.float32)
+    for t, table in enumerate((mag[...], jnp.cos(phase[...]), jnp.sin(phase[...]))):
+        tables[t] = jnp.dot(
+            table, chosen, precision=lax.Precision.HIGHEST, preferred_element_type=jnp.float32
+        )
+    tables[3] = noise[:, pl.ds(pl.multiple_of(me * width, width), width)]
+    for r in range(n):
+        loads["s", r].wait()
+
+    def reduce_step(b, j):
+        half = 1 << (bits - 1 - j)
+        for h in range(2):
+            scatter[b, h, j].wait_recv()
+            if half == 1:
+                coeff = acc[b, h, 0] + decode(code_in[b, h, 1])
+                acc[b, h, 0] = coeff
+                power_out[b, h] = jnp.sum((coeff * coeff).reshape(rows // 8, 8, HALF), axis=0)
+                continue
+            low = half // 2
+            code_out[b, h, low:half] = encode(
+                acc[b, h, low:half] + decode(code_in[b, h, half + low:2 * half])
+            )
+            send_scatter(b, h, j + 1)
+            acc[b, h, 0:low] = acc[b, h, 0:low] + decode(code_in[b, h, half:half + low])
+        if half == 1:
+            powers[b] = remote(
+                power_out.at[b], power_in.at[b], pw_send.at[b], pw_recv.at[b], other
+            )
+
+    def equalize_step(b):
+        powers[b].wait_recv()
+        for h in range(2):
+            power = jnp.sum(power_out[b, h] + power_in[b, h], axis=0, keepdims=True) / segments
+            lanes = slice(h * HALF, (h + 1) * HALF)
+            gain = power / (power + tables[3, b:b + 1, lanes]) / tables[0, b:b + 1, lanes]
+            cosine, sine = tables[1, b:b + 1, lanes], tables[2, b:b + 1, lanes]
+            real, imag = acc[b, h, 0, 0:seg_local, :], acc[b, h, 0, seg_local:rows, :]
+            gathered[b, h, 0, 0:seg_local, :] = (gain * (real * cosine + imag * sine)).astype(jnp.bfloat16)
+            gathered[b, h, 0, seg_local:rows, :] = (gain * (imag * cosine - real * sine)).astype(jnp.bfloat16)
+            send_gather(b, h, bits - 1)
+
+    def gather_step(b, j):
+        for h in range(2):
+            gather[b, h, j].wait_recv()
+            if j > 0:
+                send_gather(b, h, j - 1)
+        if j == 0:
+            beam = jnp.zeros((rows, out.shape[1]), jnp.float32)
+            for r in range(n):
+                left = jnp.concatenate([gathered[b, 0, slot(0, r)], gathered[b, 1, slot(1, r)]], axis=1)
+                beam = beam + jnp.dot(left, sbuf[r], preferred_element_type=jnp.float32)
+            beam_out[b] = jnp.sum((beam * beam).reshape(rows // 8, 8, out.shape[1]), axis=0)
+
+    for b, step in events[early:]:
+        if step == 0:
+            send_scatter(b, 0, 0)
+            send_scatter(b, 1, 0)
+        elif step <= bits:
+            reduce_step(b, step - 1)
+        elif step == bits + 1:
+            equalize_step(b)
+        else:
+            gather_step(b, 2 * bits + 1 - step)
+
+    final = remote(beam_out, beam_in, bm_send.at[0], bm_recv.at[0], other)
+    final.wait_recv()
+    for b in range(bins):
+        out[b:b + 1, :] = jnp.sum(beam_out[b] + beam_in[b], axis=0, keepdims=True) / segments
+    for copy in sends:
+        copy.wait_send()
+
+
+def fused(n, bits, pressure, harmonics, steering, radial_mag, radial_phase, noise):
+    _, bins, seg_local, mics = pressure.shape
+    rows = 2 * seg_local
+    dirs = steering.shape[1]
+    width = 2 * HALF
+    f32, bf16 = jnp.float32, jnp.bfloat16
+    dma = pltpu.SemaphoreType.DMA
+    anywhere, vmem = pl.BlockSpec(memory_space=pl.ANY), pl.BlockSpec(memory_space=pltpu.VMEM)
+    return pl.pallas_call(
+        functools.partial(kernel, n, bits, seg_local),
+        out_shape=jax.ShapeDtypeStruct((bins, dirs), f32),
+        in_specs=[anywhere] * 3 + [vmem] * 3,
+        out_specs=vmem,
+        scratch_shapes=[
+            pltpu.VMEM((rows * bins, mics), bf16),
+            pltpu.VMEM((n, mics, width), bf16),
+            pltpu.VMEM((n, width, dirs), bf16),
+            pltpu.VMEM((4, bins, width), f32),
+            pltpu.VMEM((bins, 2, n // 2, rows, HALF), f32),
+            pltpu.VMEM((bins, 2, n, rows, HALF), bf16),
+            pltpu.VMEM((bins, 2, n, rows, HALF), bf16),
+            pltpu.VMEM((bins, 2, n, rows, HALF), bf16),
+            pltpu.VMEM((bins, 2, 8, HALF), f32),
+            pltpu.VMEM((bins, 2, 8, HALF), f32),
+            pltpu.VMEM((bins, 8, dirs), f32),
+            pltpu.VMEM((bins, 8, dirs), f32),
+            dma((1 + 2 * n,)),
+            dma((bins, 2, bits)),
+            dma((bins, 2, bits)),
+            dma((bins, 2, bits)),
+            dma((bins, 2, bits)),
+            dma((bins,)),
+            dma((bins,)),
+            dma((1,)),
+            dma((1,)),
+        ],
+        compiler_params=pltpu.CompilerParams(
+            collective_id=0, has_side_effects=True, vmem_limit_bytes=44 * 2**20
+        ),
+    )(
+        pressure.reshape(rows * bins, mics), harmonics, steering,
+        radial_mag, radial_phase, noise,
+    )
+
+
 def solution(mesh):
     placed = (P(None, None, "seg", "mic"), P("mic", None), P(None, "mic"), P(), P(), P())
+    n = mesh.shape["mic"]
+    bits = n.bit_length() - 1
+
+    def run(pressure, harmonics, *rest):
+        fits = n == 1 << bits and bits >= 2 and harmonics.shape[1] == 2 * HALF * n
+        fits = fits and mesh.shape["seg"] == 2 and pressure.shape[2] % 16 == 0
+        if fits:
+            return fused(n, bits, pressure, harmonics, *rest)
+        return shards(pressure, harmonics, *rest)
+
     return jax.shard_map(
-        shards, mesh=mesh, in_specs=placed, out_specs=P(None, "mic"), check_vma=False
+        run, mesh=mesh, in_specs=placed, out_specs=P(None, "mic"), check_vma=False
     )

time: 219 us -> 69.4 us (0.32)
  waiting for transfers between devices: 186 us -> 0 us
  Pallas kernels: 0 us -> 61.6 us
  between operations: 13.5 us -> 0.02 us
  other arithmetic: 9.14 us -> 0 us
  local copies, waits for them, and re-layouts: 0.73 us -> 7.14 us
  matrix products: 6.31 us -> 0 us
  blocking collectives: 2.48 us -> 0 us
    psum x2 -> x0, waiting for transfers between devices: 186 us -> none  [the longest x1 170 us: shards(): owned = lax.psum(local_terms, 'mic')]
    pallas_call x0 -> x1, Pallas kernels: none -> 61.6 us  [fused(): pl.pallas_call(functools.partial(kernel, n, bits, seg_local), out_shape=j...]
    unnamed x8 -> x13, local copies, waits for them, and re-layouts: 0.27 us -> 7.14 us
    dot_general x2 -> x0, matrix products: 6.31 us -> none  [the longest x1 5.58 us: shards(): lax.dot_general(harmonics, flat, (((0,), (1,)), ((), ())), preferred_elem...]
    reduce_sum x4 -> x0, other arithmetic: 4.48 us -> none  [the longest x1 3.34 us: shards(): jnp.sum(coeff[:, 0] * coeff[:, 0] + coeff[:, 1] * coeff[:, 1], axis=2)]
    another operation x2 -> x0, other arithmetic: 3.05 us -> none
    psum x1 -> x0, blocking collectives: 2.48 us -> none  [shards(): total = lax.psum(local_beam, 'seg') / segments]
  transfers between devices with their start and end apart: 2 -> 0, of which waited for: 2 -> 0; matrix products, arithmetic and copies ran while one was open for 1% -> 0% of each run, Pallas kernels for 0% -> 0%
where the time goes in v1:
time: 69.4 us; the launch traced here: 68.8 us
  Pallas kernels  61.6 us (89%)
  local copies, waits for them, and re-layouts  7.14 us (10%)
    pallas_call x1, Pallas kernels, fused(): pl.pallas_call(functools.partial(kernel, n, bits, seg_local), out_shape=j...  61.6 us
    unnamed x13, local copies, waits for them, and re-layouts  7.14 us

profile of v1, /device:TPU:1, one launch (start us, length us, event | category | flops | bytes accessed | tf_op | source)
XLA Modules:
  0.0 68.8 jit_solution(3921248568866860377)
XLA Ops:
  0.0 0.0 copy-start
  0.0 2.2 %copy-done = bf16[512,4096]{1,0:T(8,128)(2,1)S(1)} copy-done((bf16[512,4096]{1,0:T(8,128)(2,1)S(1)}, bf16[512,4096]{1,0:T(8,128)(2,1)}, u32[]{:S(2)}) %copy-start) | copy-done | bytes 4194328
  2.2 0.0 copy-start.1
  2.2 1.2 %copy-done.1 = bf16[4096,128]{1,0:T(8,128)(2,1)S(1)} copy-done((bf16[4096,128]{1,0:T(8,128)(2,1)S(1)}, bf16[4096,128]{1,0:T(8,128)(2,1)}, u32[]{:S(2)}) %copy-start.1) | copy-done | bytes 1048600
  3.4 0.0 copy-start.2
  3.4 0.9 %copy-done.2 = bf16[2,4,32,512]{3,2,1,0:T(8,128)(2,1)S(1)} copy-done((bf16[2,4,32,512]{3,2,1,0:T(8,128)(2,1)S(1)}, bf16[2,4,32,512]{3,2,1,0:T(8,128)(2,1)}, u32[]{:S(2)}) %copy-start.2) | copy-done | bytes 262168
  4.4 0.0 copy-start.3
  4.4 0.8 %copy-done.3 = f32[4,4096]{1,0:T(4,128)S(1)} copy-done((f32[4,4096]{1,0:T(4,128)S(1)}, f32[4,4096]{1,0:T(4,128)}, u32[]{:S(2)}) %copy-start.3) | copy-done | bytes 65560
  5.2 0.0 copy-start.4
  5.2 0.7 copy-done.4
  5.9 0.0 copy-start.5
  5.9 0.7 copy-done.5
  6.6 61.6 %shard_map.64 = f32[4,128]{1,0:T(4,128)S(1)} custom-call(bf16[256,512]{1,0:T(8,128)(2,1)S(1)} %bitcast.1, bf16[512,4096]{1,0:T(8,128)(2,1)S(1)} %copy-done, bf16[4096,128]{1,0:T(8,128)(2,1)S(1)} %copy-done.1, f32[4,64]{1,0:T(4,128)S(1)} %copy-done.4, f32[4,64]{1,0:T(4,128)S(1)} %copy-done.5, f32[4,4096]{1,0:T(4,128)S(1)} %copy-done.3), custom_call_target="tpu_custom_call" | custom-call | tf_op jit(solution)/shard_map/pallas_call | solution.py:266
  68.2 0.6 copy.8
Async XLA Ops:
  0.0 2.2 %copy-start = (bf16[512,4096]{1,0:T(8,128)(2,1)S(1)}, bf16[512,4096]{1,0:T(8,128)(2,1)}, u32[]{:S(2)}) copy-start(bf16[512,4096]{1,0:T(8,128)(2,1)} %harmonics.1) | copy-start | bytes 12582916
  2.2 1.2 %copy-start.1 = (bf16[4096,128]{1,0:T(8,128)(2,1)S(1)}, bf16[4096,128]{1,0:T(8,128)(2,1)}, u32[]{:S(2)}) copy-start(bf16[4096,128]{1,0:T(8,128)(2,1)} %steering.1) | copy-start | bytes 3145732
  3.4 0.9 %copy-start.2 = (bf16[2,4,32,512]{3,2,1,0:T(8,128)(2,1)S(1)}, bf16[2,4,32,512]{3,2,1,0:T(8,128)(2,1)}, u32[]{:S(2)}) copy-start(bf16[2,4,32,512]{3,2,1,0:T(8,128)(2,1)} %param.6) | copy-start | bytes 786436
  4.4 0.8 %copy-start.3 = (f32[4,4096]{1,0:T(4,128)S(1)}, f32[4,4096]{1,0:T(4,128)}, u32[]{:S(2)}) copy-start(f32[4,4096]{1,0:T(4,128)} %noise.1) | copy-start | bytes 196612
  5.2 0.7 copy-start.4
  5.9 0.7 copy-start.5

commit v2 on v1

--- a/solution.py
+++ b/solution.py
@@ -9,7 +9,9 @@
 
 MESH = pl.DeviceIdType.MESH
 HALF = 128
-OFFSET = 2.5
+OFFSET = 4.0
+AHEAD = 1
+LENGTHS = (2.5, 3.5, 2.0, 3.5, 2.5, 4.0, 0.0)
 
 
 def order_lookup(table, count, start):
@@ -67,16 +69,10 @@
     return jnp.where(code < 0, -root, jnp.where(code > 0, root, 0.0))
 
 
-def schedule(bins, bits):
-    length = [2.6] + [2.0] + [1.5] * (bits - 2)
-    after = length + [1.5] + length[::-1]
-    at, events = 0.0, []
-    for step in range(len(after) + 1):
-        for b in range(bins):
-            events.append((at + OFFSET * b, -step, b))
-        if step < len(after):
-            at += after[step]
-    return [(b, -negative) for _, negative, b in sorted(events)]
+def schedule(bins):
+    starts = [sum(LENGTHS[:step]) for step in range(len(LENGTHS))]
+    events = [(starts[step] + OFFSET * b, -step, b) for step in range(len(LENGTHS)) for b in range(bins)]
+    return [(b, 1 - negative) for _, negative, b in sorted(events)]
 
 
 def kernel(
@@ -91,16 +87,17 @@
     segments = seg_local * 2
     me, core = lax.axis_index("mic"), lax.axis_index("seg")
     step_of = [(1 << b) * (1 - 2 * ((me // (1 << b)) % 2)) for b in range(bits)]
-    orders = ([0, 1] + list(range(2, bits)), [1, 0] + list(range(2, bits)))
+    rest = n // 4
 
     def owner(r):
         return me + sum(step_of[b] for b in range(bits) if (r >> b) & 1)
 
     def slot(h, r):
-        return sum(((r >> b) & 1) << (bits - 1 - j) for j, b in enumerate(orders[h]))
-
-    def near(bit):
-        return (me + step_of[bit], core)
+        x, y = r & 1, (r >> 1) & 1
+        return (r >> 2) + rest * ((2 * x + y) if h == 0 else (2 * y + x))
+
+    def near(r):
+        return (owner(r), core)
 
     other = (me, 1 - core)
 
@@ -115,8 +112,9 @@
         )
         loads["h", r].start()
     barrier = pltpu.get_barrier_semaphore()
-    for b in range(bits):
-        pl.semaphore_signal(barrier, inc=1, device_id=near(b), device_id_type=MESH)
+    peers = [1, 2] + [4 * q for q in range(1, rest)]
+    for r in peers:
+        pl.semaphore_signal(barrier, inc=1, device_id=near(r), device_id_type=MESH)
     pl.semaphore_signal(barrier, inc=1, device_id=other, device_id_type=MESH)
     for r in range(n):
         first = pl.multiple_of(owner(r) * width, width)
@@ -139,23 +137,25 @@
     scatter, gather, powers = {}, {}, {}
 
     def send_scatter(b, h, j):
-        half = 1 << (bits - 1 - j)
+        half = n >> (j + 1)
         scatter[b, h, j] = remote(
             code_out.at[b, h, pl.ds(half, half)], code_in.at[b, h, pl.ds(half, half)],
-            rs_send.at[b, h, j], rs_recv.at[b, h, j], near(orders[h][j]),
+            rs_send.at[b, h, j], rs_recv.at[b, h, j], near(1 + (h ^ j)),
         )
 
     def send_gather(b, h, j):
-        half = 1 << (bits - 1 - j)
+        half = n >> (j + 1)
         gather[b, h, j] = remote(
             gathered.at[b, h, pl.ds(0, half)], gathered.at[b, h, pl.ds(half, half)],
-            ag_send.at[b, h, j], ag_recv.at[b, h, j], near(orders[h][j]),
-        )
-
-    events = schedule(bins, bits)
-    early = 0
-    while events[early][1] == 0:
-        early += 1
+            ag_send.at[b, h, j], ag_recv.at[b, h, j], near(1 + (h ^ j)),
+        )
+
+    def send_rest(b, h, first, target, group, send_sem, recv_sem):
+        for q in range(1, rest):
+            group[b, h, 1 + q] = remote(
+                first(q), target.at[b, h, q],
+                send_sem.at[b, h, 1 + q], recv_sem.at[b, h, 1 + q], near(4 * q),
+            )
 
     loads["p"].wait()
     for count, r in enumerate(sequence):
@@ -172,11 +172,11 @@
                     else:
                         acc[b, h, where, c * seg_local:(c + 1) * seg_local, :] = block
         if count == n // 2 - 1:
-            pl.semaphore_wait(barrier, bits + 1)
-            for b, _ in events[:early]:
+            pl.semaphore_wait(barrier, len(peers) + 1)
+            for b in range(AHEAD):
                 send_scatter(b, 0, 0)
         if count == 3 * n // 4 - 1:
-            for b, _ in events[:early]:
+            for b in range(AHEAD):
                 send_scatter(b, 1, 0)
 
     index = me * width + lax.broadcasted_iota(jnp.int32, (orders_count, width), 1)
@@ -193,24 +193,31 @@
         loads["s", r].wait()
 
     def reduce_step(b, j):
-        half = 1 << (bits - 1 - j)
+        half = n >> (j + 1)
+        low = half // 2 if j == 0 else 1
         for h in range(2):
             scatter[b, h, j].wait_recv()
-            if half == 1:
-                coeff = acc[b, h, 0] + decode(code_in[b, h, 1])
-                acc[b, h, 0] = coeff
-                power_out[b, h] = jnp.sum((coeff * coeff).reshape(rows // 8, 8, HALF), axis=0)
-                continue
-            low = half // 2
+            if j == 0 and b + AHEAD < bins:
+                send_scatter(b + AHEAD, h, 0)
             code_out[b, h, low:half] = encode(
                 acc[b, h, low:half] + decode(code_in[b, h, half + low:2 * half])
             )
-            send_scatter(b, h, j + 1)
+            if j == 0:
+                send_scatter(b, h, 1)
+            else:
+                send_rest(b, h, lambda q: code_out.at[b, h, q], code_in, scatter, rs_send, rs_recv)
+        for h in range(2):
             acc[b, h, 0:low] = acc[b, h, 0:low] + decode(code_in[b, h, half:half + low])
-        if half == 1:
-            powers[b] = remote(
-                power_out.at[b], power_in.at[b], pw_send.at[b], pw_recv.at[b], other
-            )
+
+    def power_step(b):
+        for h in range(2):
+            coeff = acc[b, h, 0]
+            for q in range(1, rest):
+                scatter[b, h, 1 + q].wait_recv()
+                coeff = coeff + decode(code_in[b, h, q])
+            acc[b, h, 0] = coeff
+            power_out[b, h] = jnp.sum((coeff * coeff).reshape(rows // 8, 8, HALF), axis=0)
+        powers[b] = remote(power_out.at[b], power_in.at[b], pw_send.at[b], pw_recv.at[b], other)
 
     def equalize_step(b):
         powers[b].wait_recv()
@@ -222,30 +229,29 @@
             real, imag = acc[b, h, 0, 0:seg_local, :], acc[b, h, 0, seg_local:rows, :]
             gathered[b, h, 0, 0:seg_local, :] = (gain * (real * cosine + imag * sine)).astype(jnp.bfloat16)
             gathered[b, h, 0, seg_local:rows, :] = (gain * (imag * cosine - real * sine)).astype(jnp.bfloat16)
-            send_gather(b, h, bits - 1)
-
-    def gather_step(b, j):
-        for h in range(2):
-            gather[b, h, j].wait_recv()
-            if j > 0:
-                send_gather(b, h, j - 1)
-        if j == 0:
-            beam = jnp.zeros((rows, out.shape[1]), jnp.float32)
-            for r in range(n):
-                left = jnp.concatenate([gathered[b, 0, slot(0, r)], gathered[b, 1, slot(1, r)]], axis=1)
-                beam = beam + jnp.dot(left, sbuf[r], preferred_element_type=jnp.float32)
-            beam_out[b] = jnp.sum((beam * beam).reshape(rows // 8, 8, out.shape[1]), axis=0)
-
-    for b, step in events[early:]:
-        if step == 0:
-            send_scatter(b, 0, 0)
-            send_scatter(b, 1, 0)
-        elif step <= bits:
-            reduce_step(b, step - 1)
-        elif step == bits + 1:
-            equalize_step(b)
-        else:
-            gather_step(b, 2 * bits + 1 - step)
+            send_rest(b, h, lambda q: gathered.at[b, h, 0], gathered, gather, ag_send, ag_recv)
+
+    def forward_step(b, j):
+        for h in range(2):
+            for k in ([1] if j == 0 else range(2, 1 + rest)):
+                gather[b, h, k].wait_recv()
+            send_gather(b, h, j)
+
+    def beam_step(b):
+        for h in range(2):
+            gather[b, h, 0].wait_recv()
+        beam = jnp.zeros((rows, out.shape[1]), jnp.float32)
+        for r in range(n):
+            left = jnp.concatenate([gathered[b, 0, slot(0, r)], gathered[b, 1, slot(1, r)]], axis=1)
+            beam = beam + jnp.dot(left, sbuf[r], preferred_element_type=jnp.float32)
+        beam_out[b] = jnp.sum((beam * beam).reshape(rows // 8, 8, out.shape[1]), axis=0)
+
+    steps = (
+        None, lambda b: reduce_step(b, 0), lambda b: reduce_step(b, 1), power_step, equalize_step,
+        lambda b: forward_step(b, 1), lambda b: forward_step(b, 0), beam_step,
+    )
+    for b, step in schedule(bins):
+        steps[step](b)
 
     final = remote(beam_out, beam_in, bm_send.at[0], bm_recv.at[0], other)
     final.wait_recv()
@@ -262,7 +268,7 @@
     width = 2 * HALF
     f32, bf16 = jnp.float32, jnp.bfloat16
     dma = pltpu.SemaphoreType.DMA
-    anywhere, vmem = pl.BlockSpec(memory_space=pl.ANY), pl.BlockSpec(memory_space=pltpu.VMEM)
+    anywhere, vmem = pl.BlockSpec(memory_space=pltpu.HBM), pl.BlockSpec(memory_space=pltpu.VMEM)
     return pl.pallas_call(
         functools.partial(kernel, n, bits, seg_local),
         out_shape=jax.ShapeDtypeStruct((bins, dirs), f32),
@@ -282,10 +288,10 @@
             pltpu.VMEM((bins, 8, dirs), f32),
             pltpu.VMEM((bins, 8, dirs), f32),
             dma((1 + 2 * n,)),
-            dma((bins, 2, bits)),
-            dma((bins, 2, bits)),
-            dma((bins, 2, bits)),
-            dma((bins, 2, bits)),
+            dma((bins, 2, 1 + n // 4)),
+            dma((bins, 2, 1 + n // 4)),
+            dma((bins, 2, 1 + n // 4)),
+            dma((bins, 2, 1 + n // 4)),
             dma((bins,)),
             dma((bins,)),
             dma((1,)),
@@ -306,7 +312,7 @@
     bits = n.bit_length() - 1
 
     def run(pressure, harmonics, *rest):
-        fits = n == 1 << bits and bits >= 2 and harmonics.shape[1] == 2 * HALF * n
+        fits = n == 1 << bits and bits >= 3 and harmonics.shape[1] == 2 * HALF * n
         fits = fits and mesh.shape["seg"] == 2 and pressure.shape[2] % 16 == 0
         if fits:
             return fused(n, bits, pressure, harmonics, *rest)

time: 69.4 us -> 64 us (0.922)
  Pallas kernels: 61.6 us -> 56.5 us
    pallas_call x1, Pallas kernels: 61.6 us -> 56.5 us  [fused(): pl.pallas_call(functools.partial(kernel, n, bits, seg_local), out_shape=j...]
where the time goes in v2:
time: 64 us; the launch traced here: 63.7 us
  Pallas kernels  56.5 us (88%)
  local copies, waits for them, and re-layouts  7.14 us (11%)
    pallas_call x1, Pallas kernels, fused(): pl.pallas_call(functools.partial(kernel, n, bits, seg_local), out_shape=j...  56.5 us
    unnamed x13, local copies, waits for them, and re-layouts  7.14 us

profile of v2, /device:TPU:1, one launch (start us, length us, event | category | flops | bytes accessed | tf_op | source)
XLA Modules:
  0.0 63.7 jit_solution(12327935277693355156)
XLA Ops:
  0.0 0.0 copy-start
  0.0 2.2 %copy-done = bf16[512,4096]{1,0:T(8,128)(2,1)S(1)} copy-done((bf16[512,4096]{1,0:T(8,128)(2,1)S(1)}, bf16[512,4096]{1,0:T(8,128)(2,1)}, u32[]{:S(2)}) %copy-start) | copy-done | bytes 4194328
  2.2 0.0 copy-start.1
  2.2 1.2 %copy-done.1 = bf16[4096,128]{1,0:T(8,128)(2,1)S(1)} copy-done((bf16[4096,128]{1,0:T(8,128)(2,1)S(1)}, bf16[4096,128]{1,0:T(8,128)(2,1)}, u32[]{:S(2)}) %copy-start.1) | copy-done | bytes 1048600
  3.4 0.0 copy-start.2
  3.4 0.9 %copy-done.2 = bf16[2,4,32,512]{3,2,1,0:T(8,128)(2,1)S(1)} copy-done((bf16[2,4,32,512]{3,2,1,0:T(8,128)(2,1)S(1)}, bf16[2,4,32,512]{3,2,1,0:T(8,128)(2,1)}, u32[]{:S(2)}) %copy-start.2) | copy-done | bytes 262168
  4.4 0.0 copy-start.3
  4.4 0.8 %copy-done.3 = f32[4,4096]{1,0:T(4,128)S(1)} copy-done((f32[4,4096]{1,0:T(4,128)S(1)}, f32[4,4096]{1,0:T(4,128)}, u32[]{:S(2)}) %copy-start.3) | copy-done | bytes 65560
  5.2 0.0 copy-start.4
  5.2 0.7 %copy-done.4 = f32[4,64]{1,0:T(4,128)S(1)} copy-done((f32[4,64]{1,0:T(4,128)S(1)}, f32[4,64]{1,0:T(4,128)}, u32[]{:S(2)}) %copy-start.4) | copy-done | bytes 1048
  5.9 0.0 copy-start.5
  5.9 0.7 %copy-done.5 = f32[4,64]{1,0:T(4,128)S(1)} copy-done((f32[4,64]{1,0:T(4,128)S(1)}, f32[4,64]{1,0:T(4,128)}, u32[]{:S(2)}) %copy-start.5) | copy-done | bytes 1048
  6.6 56.5 %shard_map.64 = f32[4,128]{1,0:T(4,128)S(1)} custom-call(bf16[256,512]{1,0:T(8,128)(2,1)S(1)} %bitcast.1, bf16[512,4096]{1,0:T(8,128)(2,1)S(1)} %copy-done, bf16[4096,128]{1,0:T(8,128)(2,1)S(1)} %copy-done.1, f32[4,64]{1,0:T(4,128)S(1)} %copy-done.4, f32[4,64]{1,0:T(4,128)S(1)} %copy-done.5, f32[4,4096]{1,0:T(4,128)S(1)} %copy-done.3), custom_call_target="tpu_custom_call" | custom-call | tf_op jit(solution)/shard_map/pallas_call | solution.py:272
  63.1 0.6 copy.8
Async XLA Ops:
  0.0 2.2 %copy-start = (bf16[512,4096]{1,0:T(8,128)(2,1)S(1)}, bf16[512,4096]{1,0:T(8,128)(2,1)}, u32[]{:S(2)}) copy-start(bf16[512,4096]{1,0:T(8,128)(2,1)} %harmonics.1) | copy-start | bytes 12582916
  2.2 1.2 %copy-start.1 = (bf16[4096,128]{1,0:T(8,128)(2,1)S(1)}, bf16[4096,128]{1,0:T(8,128)(2,1)}, u32[]{:S(2)}) copy-start(bf16[4096,128]{1,0:T(8,128)(2,1)} %steering.1) | copy-start | bytes 3145732
  3.4 0.9 %copy-start.2 = (bf16[2,4,32,512]{3,2,1,0:T(8,128)(2,1)S(1)}, bf16[2,4,32,512]{3,2,1,0:T(8,128)(2,1)}, u32[]{:S(2)}) copy-start(bf16[2,4,32,512]{3,2,1,0:T(8,128)(2,1)} %param.6) | copy-start | bytes 786436
  4.4 0.8 %copy-start.3 = (f32[4,4096]{1,0:T(4,128)S(1)}, f32[4,4096]{1,0:T(4,128)}, u32[]{:S(2)}) copy-start(f32[4,4096]{1,0:T(4,128)} %noise.1) | copy-start | bytes 196612
  5.2 0.7 %copy-start.4 = (f32[4,64]{1,0:T(4,128)S(1)}, f32[4,64]{1,0:T(4,128)}, u32[]{:S(2)}) copy-start(f32[4,64]{1,0:T(4,128)} %mag.1) | copy-start | bytes 3076
  5.9 0.7 %copy-start.5 = (f32[4,64]{1,0:T(4,128)S(1)}, f32[4,64]{1,0:T(4,128)}, u32[]{:S(2)}) copy-start(f32[4,64]{1,0:T(4,128)} %phase.1) | copy-start | bytes 3076

commit v3 on v2

--- a/solution.py
+++ b/solution.py
@@ -9,9 +9,19 @@
 
 MESH = pl.DeviceIdType.MESH
 HALF = 128
-OFFSET = 4.0
-AHEAD = 1
-LENGTHS = (2.5, 3.5, 2.0, 3.5, 2.5, 4.0, 0.0)
+BINS = 4
+STEPS = (
+    "0a 1a 0b 01",
+    "11 1b 2a 02",
+    "3a 12 2b 21",
+    "03 04 13 31",
+    "14 3b 22 05",
+    "06 32 15 23",
+    "24 1g 0g 33",
+    "16 34 25 2g",
+    "35 26 07 3g",
+    "36 27 17 37",
+)
 
 
 def order_lookup(table, count, start):
@@ -69,20 +79,14 @@
     return jnp.where(code < 0, -root, jnp.where(code > 0, root, 0.0))
 
 
-def schedule(bins):
-    starts = [sum(LENGTHS[:step]) for step in range(len(LENGTHS))]
-    events = [(starts[step] + OFFSET * b, -step, b) for step in range(len(LENGTHS)) for b in range(bins)]
-    return [(b, 1 - negative) for _, negative, b in sorted(events)]
-
-
 def kernel(
     n, bits, seg_local,
-    pressure, harmonics, steering, mag, phase, noise, out,
-    pbuf, hbuf, sbuf, tables, acc, code_out, code_in, gathered,
+    pressure, harmonics, steering, mag_far, phase_far, noise_far, out,
+    pbuf, hbuf, sbuf, mag, phase, noise, tables, acc, code_out, code_in, gathered,
     power_out, power_in, beam_out, beam_in,
     local_sem, rs_send, rs_recv, ag_send, ag_recv, pw_send, pw_recv, bm_send, bm_recv,
 ):
-    bins, orders_count = mag.shape
+    bins, orders_count = mag_far.shape
     rows = 2 * seg_local
     segments = seg_local * 2
     me, core = lax.axis_index("mic"), lax.axis_index("seg")
@@ -111,6 +115,13 @@
             harmonics.at[:, pl.ds(first, width)], hbuf.at[r], local_sem.at[1 + r]
         )
         loads["h", r].start()
+    small = []
+    first = pl.multiple_of(me * width, width)
+    for i, (src, dst) in enumerate(
+        ((mag_far, mag), (phase_far, phase), (noise_far.at[:, pl.ds(first, width)], noise))
+    ):
+        small.append(pltpu.make_async_copy(src, dst, local_sem.at[1 + 2 * n + i]))
+        small[-1].start()
     barrier = pltpu.get_barrier_semaphore()
     peers = [1, 2] + [4 * q for q in range(1, rest)]
     for r in peers:
@@ -136,26 +147,41 @@
 
     scatter, gather, powers = {}, {}, {}
 
-    def send_scatter(b, h, j):
-        half = n >> (j + 1)
-        scatter[b, h, j] = remote(
-            code_out.at[b, h, pl.ds(half, half)], code_in.at[b, h, pl.ds(half, half)],
-            rs_send.at[b, h, j], rs_recv.at[b, h, j], near(1 + (h ^ j)),
-        )
-
-    def send_gather(b, h, j):
-        half = n >> (j + 1)
-        gather[b, h, j] = remote(
-            gathered.at[b, h, pl.ds(0, half)], gathered.at[b, h, pl.ds(half, half)],
-            ag_send.at[b, h, j], ag_recv.at[b, h, j], near(1 + (h ^ j)),
+    quarter, half = n // 4, n // 2
+
+    def send_scatter(b, h, j, name, first):
+        piece = pl.ds(first, quarter)
+        scatter[b, h, name] = remote(
+            code_out.at[b, h, piece], code_in.at[b, h, piece],
+            rs_send.at[b, h, name], rs_recv.at[b, h, name], near(1 + (h ^ j)),
+        )
+
+    def send_gather(b, h, j, name, first):
+        gather[b, h, name] = remote(
+            gathered.at[b, h, pl.ds(first, quarter)],
+            gathered.at[b, h, pl.ds(first + (half >> j), quarter)],
+            ag_send.at[b, h, name], ag_recv.at[b, h, name], near(1 + (h ^ j)),
         )
 
     def send_rest(b, h, first, target, group, send_sem, recv_sem):
         for q in range(1, rest):
-            group[b, h, 1 + q] = remote(
+            group[b, h, 2 + q] = remote(
                 first(q), target.at[b, h, q],
-                send_sem.at[b, h, 1 + q], recv_sem.at[b, h, 1 + q], near(4 * q),
+                send_sem.at[b, h, 2 + q], recv_sem.at[b, h, 2 + q], near(4 * q),
             )
+
+    events = " ".join(STEPS).split()
+    events = [(int(event[0]), event[1]) for event in events]
+    early = 0
+    while events[early][1] in "ab":
+        early += 1
+
+    def first_step(b, h, name):
+        send_scatter(b, h, 0, "ab".index(name), half + quarter if name == "a" else half)
+
+    def early_steps(h):
+        for b, name in events[:early]:
+            first_step(b, h, name)
 
     loads["p"].wait()
     for count, r in enumerate(sequence):
@@ -173,12 +199,12 @@
                         acc[b, h, where, c * seg_local:(c + 1) * seg_local, :] = block
         if count == n // 2 - 1:
             pl.semaphore_wait(barrier, len(peers) + 1)
-            for b in range(AHEAD):
-                send_scatter(b, 0, 0)
+            early_steps(0)
         if count == 3 * n // 4 - 1:
-            for b in range(AHEAD):
-                send_scatter(b, 1, 0)
-
+            early_steps(1)
+
+    for load in small:
+        load.wait()
     index = me * width + lax.broadcasted_iota(jnp.int32, (orders_count, width), 1)
     order = lax.broadcasted_iota(jnp.int32, (orders_count, width), 0)
     last = order == orders_count - 1
@@ -188,32 +214,36 @@
         tables[t] = jnp.dot(
             table, chosen, precision=lax.Precision.HIGHEST, preferred_element_type=jnp.float32
         )
-    tables[3] = noise[:, pl.ds(pl.multiple_of(me * width, width), width)]
+    tables[3] = noise[...]
     for r in range(n):
         loads["s", r].wait()
 
-    def reduce_step(b, j):
-        half = n >> (j + 1)
-        low = half // 2 if j == 0 else 1
-        for h in range(2):
-            scatter[b, h, j].wait_recv()
-            if j == 0 and b + AHEAD < bins:
-                send_scatter(b + AHEAD, h, 0)
-            code_out[b, h, low:half] = encode(
-                acc[b, h, low:half] + decode(code_in[b, h, half + low:2 * half])
+    def reduce_first(b):
+        for h in range(2):
+            scatter[b, h, 0].wait_recv()
+            code_out[b, h, quarter:half] = encode(
+                acc[b, h, quarter:half] + decode(code_in[b, h, half + quarter:n])
             )
-            if j == 0:
-                send_scatter(b, h, 1)
-            else:
-                send_rest(b, h, lambda q: code_out.at[b, h, q], code_in, scatter, rs_send, rs_recv)
-        for h in range(2):
-            acc[b, h, 0:low] = acc[b, h, 0:low] + decode(code_in[b, h, half:half + low])
+            send_scatter(b, h, 1, 2, quarter)
+
+    def reduce_second(b):
+        for h in range(2):
+            scatter[b, h, 1].wait_recv()
+            acc[b, h, 0:quarter] = acc[b, h, 0:quarter] + decode(code_in[b, h, half:half + quarter])
+        for h in range(2):
+            scatter[b, h, 2].wait_recv()
+            code_out[b, h, 1:quarter] = encode(
+                acc[b, h, 1:quarter] + decode(code_in[b, h, quarter + 1:half])
+            )
+            send_rest(b, h, lambda q: code_out.at[b, h, q], code_in, scatter, rs_send, rs_recv)
+        for h in range(2):
+            acc[b, h, 0] = acc[b, h, 0] + decode(code_in[b, h, quarter])
 
     def power_step(b):
         for h in range(2):
             coeff = acc[b, h, 0]
             for q in range(1, rest):
-                scatter[b, h, 1 + q].wait_recv()
+                scatter[b, h, 2 + q].wait_recv()
                 coeff = coeff + decode(code_in[b, h, q])
             acc[b, h, 0] = coeff
             power_out[b, h] = jnp.sum((coeff * coeff).reshape(rows // 8, 8, HALF), axis=0)
@@ -231,27 +261,41 @@
             gathered[b, h, 0, seg_local:rows, :] = (gain * (imag * cosine - real * sine)).astype(jnp.bfloat16)
             send_rest(b, h, lambda q: gathered.at[b, h, 0], gathered, gather, ag_send, ag_recv)
 
-    def forward_step(b, j):
-        for h in range(2):
-            for k in ([1] if j == 0 else range(2, 1 + rest)):
-                gather[b, h, k].wait_recv()
-            send_gather(b, h, j)
+    def forward_first(b):
+        for h in range(2):
+            for q in range(1, rest):
+                gather[b, h, 2 + q].wait_recv()
+            send_gather(b, h, 1, 2, 0)
+
+    def forward_own(b):
+        for h in range(2):
+            send_gather(b, h, 0, 0, 0)
+
+    def forward_second(b):
+        for h in range(2):
+            gather[b, h, 2].wait_recv()
+            send_gather(b, h, 0, 1, quarter)
 
     def beam_step(b):
         for h in range(2):
             gather[b, h, 0].wait_recv()
+            gather[b, h, 1].wait_recv()
         beam = jnp.zeros((rows, out.shape[1]), jnp.float32)
         for r in range(n):
             left = jnp.concatenate([gathered[b, 0, slot(0, r)], gathered[b, 1, slot(1, r)]], axis=1)
             beam = beam + jnp.dot(left, sbuf[r], preferred_element_type=jnp.float32)
         beam_out[b] = jnp.sum((beam * beam).reshape(rows // 8, 8, out.shape[1]), axis=0)
 
-    steps = (
-        None, lambda b: reduce_step(b, 0), lambda b: reduce_step(b, 1), power_step, equalize_step,
-        lambda b: forward_step(b, 1), lambda b: forward_step(b, 0), beam_step,
-    )
-    for b, step in schedule(bins):
-        steps[step](b)
+    steps = {
+        "1": reduce_first, "2": reduce_second, "3": power_step, "4": equalize_step,
+        "5": forward_first, "g": forward_own, "6": forward_second, "7": beam_step,
+    }
+    for b, name in events[early:]:
+        if name in steps:
+            steps[name](b)
+        else:
+            first_step(b, 0, name)
+            first_step(b, 1, name)
 
     final = remote(beam_out, beam_in, bm_send.at[0], bm_recv.at[0], other)
     final.wait_recv()
@@ -272,12 +316,15 @@
     return pl.pallas_call(
         functools.partial(kernel, n, bits, seg_local),
         out_shape=jax.ShapeDtypeStruct((bins, dirs), f32),
-        in_specs=[anywhere] * 3 + [vmem] * 3,
+        in_specs=[anywhere] * 6,
         out_specs=vmem,
         scratch_shapes=[
             pltpu.VMEM((rows * bins, mics), bf16),
             pltpu.VMEM((n, mics, width), bf16),
             pltpu.VMEM((n, width, dirs), bf16),
+            pltpu.VMEM(radial_mag.shape, f32),
+            pltpu.VMEM(radial_mag.shape, f32),
+            pltpu.VMEM((bins, width), f32),
             pltpu.VMEM((4, bins, width), f32),
             pltpu.VMEM((bins, 2, n // 2, rows, HALF), f32),
             pltpu.VMEM((bins, 2, n, rows, HALF), bf16),
@@ -287,18 +334,18 @@
             pltpu.VMEM((bins, 2, 8, HALF), f32),
             pltpu.VMEM((bins, 8, dirs), f32),
             pltpu.VMEM((bins, 8, dirs), f32),
-            dma((1 + 2 * n,)),
-            dma((bins, 2, 1 + n // 4)),
-            dma((bins, 2, 1 + n // 4)),
-            dma((bins, 2, 1 + n // 4)),
-            dma((bins, 2, 1 + n // 4)),
+            dma((4 + 2 * n,)),
+            dma((bins, 2, 2 + n // 4)),
+            dma((bins, 2, 2 + n // 4)),
+            dma((bins, 2, 2 + n // 4)),
+            dma((bins, 2, 2 + n // 4)),
             dma((bins,)),
             dma((bins,)),
             dma((1,)),
             dma((1,)),
         ],
         compiler_params=pltpu.CompilerParams(
-            collective_id=0, has_side_effects=True, vmem_limit_bytes=44 * 2**20
+            collective_id=0, has_side_effects=True, vmem_limit_bytes=63 * 2**20
         ),
     )(
         pressure.reshape(rows * bins, mics), harmonics, steering,
@@ -312,7 +359,7 @@
     bits = n.bit_length() - 1
 
     def run(pressure, harmonics, *rest):
-        fits = n == 1 << bits and bits >= 3 and harmonics.shape[1] == 2 * HALF * n
+        fits = n == 1 << bits and bits >= 3 and pressure.shape[1] == BINS and harmonics.shape[1] == 2 * HALF * n
         fits = fits and mesh.shape["seg"] == 2 and pressure.shape[2] % 16 == 0
         if fits:
             return fused(n, bits, pressure, harmonics, *rest)

time: 64 us -> 53.8 us (0.84)
  local copies, waits for them, and re-layouts: 7.14 us -> 1.26 us
  Pallas kernels: 56.5 us -> 52.3 us
    unnamed x13 -> x1, local copies, waits for them, and re-layouts: 7.14 us -> 1.26 us
    pallas_call x1, Pallas kernels: 56.5 us -> 52.3 us  [fused(): pl.pallas_call(functools.partial(kernel, n, bits, seg_local), out_shape=j...]
where the time goes in v3:
time: 53.8 us; the launch traced here: 53.6 us
  Pallas kernels  52.3 us (97%)
  local copies, waits for them, and re-layouts  1.26 us (2%)
    pallas_call x1, Pallas kernels, fused(): pl.pallas_call(functools.partial(kernel, n, bits, seg_local), out_shape=j...  52.3 us
    unnamed x1, local copies, waits for them, and re-layouts  1.26 us

profile of v3, /device:TPU:1, one launch (start us, length us, event | category | flops | bytes accessed | tf_op | source)
XLA Modules:
  0.0 53.6 jit_solution(7826457756568490078)
XLA Ops:
  0.0 52.3 %shard_map.64 = f32[4,128]{1,0:T(4,128)} custom-call(bf16[256,512]{1,0:T(8,128)(2,1)} %bitcast.1, bf16[512,4096]{1,0:T(8,128)(2,1)} %harmonics.1, bf16[4096,128]{1,0:T(8,128)(2,1)} %steering.1, f32[4,64]{1,0:T(4,128)} %mag_far.1, f32[4,64]{1,0:T(4,128)} %phase_far.1, f32[4,4096]{1,0:T(4,128)} %noise_far.1), custom_call_target="tpu_custom_call" | custom-call | tf_op jit(solution)/shard_map/pallas_call | solution.py:316
  52.3 1.3 %copy.8 = f32[4,128]{1,0:T(4,128)} copy(f32[4,128]{1,0:T(4,128)} %shard_map.64) | data formatting | bytes 4096
